TPU v7x, 32 devices: a whole 2x2x4 slice. The times are simulated.
32 devices in a mesh: rows: 16 (over z, y, x), tm: 2 (over core).
Axes of the slice: x: 2, y: 2, z: 4, core: 2. Of those that a mesh axis runs over, the one named last changes fastest.
Arguments:
- snapshots: bfloat16 [262144, 256], P('rows', 'tm'), may hold values from -6 to 6
- basis: bfloat16 [262144, 32], P(('rows', 'tm')), may hold values from -0.01171875 to 0.01171875
Outputs:
- gram: float32 [560, 560], replicated
- rhs: float32 [560, 32], replicated
All inputs are finite; a program needn't handle non-finite values.
Results may differ from a plain program's by a relative error of at most 0.0003.
Values may be sent and summed in bfloat16 or wider, within the bound.
A program may use at most 64 MiB of HBM per device.

v0:
```python
import jax
import jax.numpy as jnp
import numpy as np
from jax import lax
from jax.sharding import PartitionSpec as P


def from_behind(block, axis, distance):
    devices = range(lax.axis_size(axis))
    route = [(i - distance, i) for i in devices if i - distance in devices]
    return lax.ppermute(block, axis, route)


def build_sums(projected, velocity, first_step, total_steps):
    series = projected.T
    num_modes = series.shape[1]
    weight = (first_step + jnp.arange(series.shape[0]) < total_steps - 1).astype(jnp.float32)
    upper_pair = np.triu_indices(num_modes)
    quadratic = series[:, upper_pair[0]] * series[:, upper_pair[1]]
    features = jnp.concatenate([series, quadratic], axis=1)
    weighted = features * weight[:, None]
    gram_part = jnp.dot(weighted.T, features, precision=lax.Precision.HIGHEST)
    rhs_part = jnp.dot(weighted.T, velocity.T, precision=lax.Precision.HIGHEST)
    return (gram_part, rhs_part)


def shards(snapshots, basis):
    rows_count, step_count = snapshots.shape
    partial_value = jnp.einsum(
        "nr,nt->rt",
        lax.all_gather(basis, "tm", axis=0, tiled=True),
        snapshots,
        preferred_element_type=jnp.float32,
    )
    first_next = from_behind(partial_value[:, :1], "tm", -1)
    velocity_part = jnp.concatenate([partial_value[:, 1:], first_next], axis=1) - partial_value
    group_size = lax.axis_size("rows")
    share = step_count // group_size
    total_steps = step_count * lax.axis_size("tm")
    first_step = lax.axis_index("tm") * step_count + lax.axis_index("rows") * share
    whole_proj, whole_vel = lax.psum((partial_value, velocity_part), "rows")
    column = lax.axis_index("rows") * share
    projected = lax.dynamic_slice_in_dim(whole_proj, column, share, 1)
    velocity = lax.dynamic_slice_in_dim(whole_vel, column, share, 1)
    gram_part, rhs_part = build_sums(projected, velocity, first_step, total_steps)
    gram_sum, rhs_sum = lax.psum((gram_part, rhs_part), ("rows", "tm"))
    return (gram_sum / total_steps, rhs_sum / total_steps)


def solution(mesh):
    in_specs = (P("rows", "tm"), P(("rows", "tm"), None))
    out_specs = (P(), P())
    return jax.shard_map(shards, mesh=mesh, in_specs=in_specs, out_specs=out_specs, check_vma=False)
```

profile of v0, /device:TPU:0, one launch (start us, length us, event | category | flops | bytes accessed | tf_op | source)
XLA Modules:
  0.0 249.2 jit_solution(8498607268534217137)
XLA Ops:
  7.2 0.0 all-gather.2.cloned.1.call-start
  7.2 0.7 all-gather.2.cloned.1.call-update
  7.9 0.0 all-reduce.4.cloned.1.call-start
  8.0 0.7 pad_clamp_fusion.1
  8.7 0.7 pad_clamp_fusion
  9.4 12.0 %all-gather.2.cloned.1.call-done = bf16[16384,32]{0,1:T(8,128)(2,1)} async-done(((bf16[8192,32]{0,1:T(8,128)(2,1)}), bf16[16384,32]{0,1:T(8,128)(2,1)}) %all-gather.2.cloned.1.call-update) | async-done | bytes 1048592 | tf_op jit(solution)/shard_map/all_gather | solution.py:31
  21.3 3.3 %fusion.10 = f32[32,128]{1,0:T(8,128)S(1)} fusion(bf16[16384,32]{0,1:T(8,128)(2,1)} %all-gather.2.cloned.1.call-done, bf16[16384,128]{1,0:T(8,128)(2,1)} %param.6), kind=kOutput, calls=%fused_computation.21 | convolution fusion | flops 134217728 | bytes 5259264 | tf_op jit(solution)/shard_map/nr,nt->rt/dot_general | solution.py:29
  24.6 1.3 collective-permute-start
  25.9 0.1 slice.12
  25.9 1.7 collective-permute-done
  27.7 0.1 maximum_subtract_fusion
  27.7 77.0 %all-reduce.1 = (f32[32,128]{1,0:T(8,128)S(1)}, f32[32,128]{1,0:T(8,128)S(1)}) all-reduce(f32[32,128]{1,0:T(8,128)S(1)} %fusion.10, f32[32,128]{1,0:T(8,128)S(1)} %maximum_subtract_fusion), channel_id=1, replica_groups=mesh['rows'=16,'tm'=2] {'rows'}, use_global_device_ids=true, to_apply=%region_0.0 | all-reduce | flops 8192 | bytes 65536 | tf_op jit(solution)/shard_map/psum | solution.py:41
  104.7 0.1 dynamic-slice_bitcast_fusion
  104.8 0.1 copy.8
  104.9 1.6 gather_fusion.1
  106.5 1.6 gather_fusion
  108.1 0.1 copy.9
  108.2 2.6 %fusion.2 = f32[560,560]{1,0:T(8,128)} fusion(f32[8,528]{1,0:T(8,128)S(1)} %copy.9, f32[8,32]{1,0:T(8,128)S(1)} %copy.8, f32[8]{0:T(128)S(1)} %compare_convert_fusion), kind=kOutput, calls=%fused_computation.7 | convolution fusion | flops 30119040 | bytes 1272352 | tf_op jit(solution)/shard_map/dot_general | solution.py:22
  110.8 0.9 fusion
  111.7 0.0 all-reduce.4.cloned.1.call-update
  111.7 127.4 %all-reduce.4.cloned.1.call-done = (f32[560,560]{1,0:T(8,128)}, f32[560,32]{0,1:T(8,128)}) async-done(((f32[560,560]{1,0:T(8,128)}, f32[560,32]{0,1:T(8,128)}), (f32[560,560]{1,0:T(8,128)}, f32[560,32]{0,1:T(8,128)})) %all-reduce.4.cloned.1.call-update) | async-done | bytes 1326096 | tf_op jit(solution)/shard_map/psum | solution.py:46
  239.1 0.0 copy-start
  239.1 2.6 %broadcast_multiply_fusion = f32[560,560]{1,0:T(8,128)} fusion(f32[560,560]{1,0:T(8,128)} %get-tuple-element.2), kind=kLoop, calls=%fused_computation.2 | loop fusion | flops 313600 | bytes 2508800 | tf_op jit(solution)/shard_map/div | solution.py:47
  241.7 0.0 copy-done
  241.7 0.6 broadcast_multiply_fusion.1
  (2 shorter events, 0.0 us)
Async XLA Ops:
  7.2 14.1 %all-gather.2.cloned.1.call-start = ((), (), s32[]{:S(2)}) async-start(), calls=%async_computation | async-start | bytes 1572864 | tf_op jit(solution)/shard_map/all_gather | solution.py:31
  7.9 231.2 %all-reduce.4.cloned.1.call-start = ((), (), s32[]{:S(2)}) async-start(), calls=%async_computation.1 | async-start | bytes 3031040 | tf_op jit(solution)/shard_map/psum | solution.py:46
  24.6 3.1 %collective-permute-start = (f32[32,1]{1,0:T(8,128)S(1)}, f32[32,1]{1,0:T(8,128)S(1)}, u32[]{:S(2)}, u32[]{:S(2)}) collective-permute-start(f32[32,1]{1,0:T(8,128)S(1)} %bitcast.7), channel_id=1, source_target_pairs={{1,0},{3,2},{5,4},{7,6},{9,8},{11,10},{13,12},{15,14},{17,16},{19,... | collective-permute-start | bytes 392 | tf_op jit(solution)/shard_map/ppermute | solution.py:11
  239.1 2.6 %copy-start = (f32[560,32]{0,1:T(8,128)S(1)}, f32[560,32]{0,1:T(8,128)}, u32[]{:S(2)}) copy-start(f32[560,32]{0,1:T(8,128)} %get-tuple-element.3) | copy-start | bytes 215044
Sparse Core Ops, SparseCore 0:
  9.5 11.7 all-gather.1
  111.8 127.2 all-reduce.3
where the time goes:
time: 249 us
  waiting for transfers between devices  142 us (57%)
  blocking collectives  77 us (31%)
  between operations  14.1 us (6%)
  matrix products  6.72 us (3%)
  other arithmetic  4.73 us (2%)
  local copies, waits for them, and re-layouts  3.5 us (1%)
    psum x1, waiting for transfers between devices, shards(): gram_sum, rhs_sum = lax.psum((gram_part, rhs_part), ('rows', 'tm'))  127 us
    psum x1, blocking collectives, shards(): whole_proj, whole_vel = lax.psum((partial_value, velocity_part), 'rows')  77 us
    all_gather x1, waiting for transfers between devices, shards(): lax.all_gather(basis, 'tm', axis=0, tiled=True)  12 us
  transfers between devices with their start and end apart: 3, of which 3 were waited for; matrix products, arithmetic and copies ran while one was open for 1% of the time, Pallas kernels for 0%

commit v1 on v0

--- a/solution.py
+++ b/solution.py
@@ -43,7 +43,7 @@
     projected = lax.dynamic_slice_in_dim(whole_proj, column, share, 1)
     velocity = lax.dynamic_slice_in_dim(whole_vel, column, share, 1)
     gram_part, rhs_part = build_sums(projected, velocity, first_step, total_steps)
-    gram_sum, rhs_sum = lax.psum((gram_part, rhs_part), ("rows", "tm"))
+    gram_sum, rhs_sum = lax.psum(lax.psum((gram_part, rhs_part), "tm"), "rows")
     return (gram_sum / total_steps, rhs_sum / total_steps)
 
 

time: 249 us -> 262 us (1.052)
  waiting for transfers between devices: 142 us -> 155 us
    psum x1 -> x2, waiting for transfers between devices: 127 us -> 141 us  [shards(): gram_sum, rhs_sum = lax.psum(lax.psum((gram_part, rhs_part), 'tm'), 'rows')]
  transfers between devices with their start and end apart: 3 -> 4, of which waited for: 3 -> 4; matrix products, arithmetic and copies ran while one was open for 1% -> 1% of each run, Pallas kernels for 0% -> 0%
where the time goes in v1:
time: 262 us
  waiting for transfers between devices  155 us (59%)
  blocking collectives  77 us (29%)
  between operations  13.8 us (5%)
  matrix products  6.72 us (3%)
  other arithmetic  4.73 us (2%)
  local copies, waits for them, and re-layouts  3.5 us (1%)
    psum x2, waiting for transfers between devices, shards(): gram_sum, rhs_sum = lax.psum(lax.psum((gram_part, rhs_part), 'tm'), 'rows')  141 us
    psum x1, blocking collectives, shards(): whole_proj, whole_vel = lax.psum((partial_value, velocity_part), 'rows')  77 us
    all_gather x1, waiting for transfers between devices, shards(): lax.all_gather(basis, 'tm', axis=0, tiled=True)  12 us
  transfers between devices with their start and end apart: 4, of which 4 were waited for; matrix products, arithmetic and copies ran while one was open for 1% of the time, Pallas kernels for 0%

profile of v1, /device:TPU:0, one launch (start us, length us, event | category | flops | bytes accessed | tf_op | source)
XLA Modules:
  0.0 262.2 jit_solution(1552404764944095701)
XLA Ops:
  7.2 0.0 all-gather.2.cloned.1.call-start
  7.2 0.7 all-gather.2.cloned.1.call-update
  7.9 0.0 all-reduce.8.cloned.1.call-start
  8.0 0.7 pad_clamp_fusion.1
  8.7 0.7 pad_clamp_fusion
  9.4 12.0 %all-gather.2.cloned.1.call-done = bf16[16384,32]{0,1:T(8,128)(2,1)} async-done(((bf16[8192,32]{0,1:T(8,128)(2,1)}), bf16[16384,32]{0,1:T(8,128)(2,1)}) %all-gather.2.cloned.1.call-update) | async-done | bytes 1048592 | tf_op jit(solution)/shard_map/all_gather | solution.py:31
  21.3 3.3 %fusion.10 = f32[32,128]{1,0:T(8,128)S(1)} fusion(bf16[16384,32]{0,1:T(8,128)(2,1)} %all-gather.2.cloned.1.call-done, bf16[16384,128]{1,0:T(8,128)(2,1)} %param.6), kind=kOutput, calls=%fused_computation.21 | convolution fusion | flops 134217728 | bytes 5259264 | tf_op jit(solution)/shard_map/nr,nt->rt/dot_general | solution.py:29
  24.6 1.3 collective-permute-start
  25.9 0.1 slice.12
  25.9 1.7 collective-permute-done
  27.7 0.1 maximum_subtract_fusion
  27.7 77.0 %all-reduce = (f32[32,128]{1,0:T(8,128)S(1)}, f32[32,128]{1,0:T(8,128)S(1)}) all-reduce(f32[32,128]{1,0:T(8,128)S(1)} %fusion.10, f32[32,128]{1,0:T(8,128)S(1)} %maximum_subtract_fusion), channel_id=1, replica_groups=mesh['rows'=16,'tm'=2] {'rows'}, use_global_device_ids=true, to_apply=%region_0.0 | all-reduce | flops 8192 | bytes 65536 | tf_op jit(solution)/shard_map/psum | solution.py:41
  104.7 0.1 dynamic-slice_bitcast_fusion
  104.8 0.1 copy.8
  104.9 1.6 gather_fusion.1
  106.5 1.6 gather_fusion
  108.1 0.1 copy.9
  108.2 2.6 fusion.2
  110.8 0.9 fusion
  111.7 0.0 all-reduce.8.cloned.1.call-update
  111.7 0.0 all-reduce.6.cloned.1.call-start
  111.7 16.4 %all-reduce.8.cloned.1.call-done = (f32[560,560]{1,0:T(8,128)}, f32[560,32]{0,1:T(8,128)}) async-done(((f32[560,560]{1,0:T(8,128)}, f32[560,32]{0,1:T(8,128)}), (f32[560,560]{1,0:T(8,128)}, f32[560,32]{0,1:T(8,128)})) %all-reduce.8.cloned.1.call-update) | async-done | bytes 1326096 | tf_op jit(solution)/shard_map/psum | solution.py:46
  128.1 0.0 all-reduce.6.cloned.1.call-update
  128.1 124.3 %all-reduce.6.cloned.1.call-done = (f32[560,560]{1,0:T(8,128)}, f32[560,32]{0,1:T(8,128)}) async-done(((f32[560,560]{1,0:T(8,128)}, f32[560,32]{0,1:T(8,128)}), (f32[560,560]{1,0:T(8,128)}, f32[560,32]{0,1:T(8,128)})) %all-reduce.6.cloned.1.call-update) | async-done | bytes 1326096 | tf_op jit(solution)/shard_map/psum | solution.py:46
  252.4 0.0 copy-start
  252.4 2.6 broadcast_multiply_fusion
  255.0 0.0 copy-done
  255.0 0.6 broadcast_multiply_fusion.1
  (2 shorter events, 0.0 us)
Async XLA Ops:
  7.2 14.1 %all-gather.2.cloned.1.call-start = ((), (), s32[]{:S(2)}) async-start(), calls=%async_computation | async-start | bytes 1572864 | tf_op jit(solution)/shard_map/all_gather | solution.py:31
  7.9 120.2 %all-reduce.8.cloned.1.call-start = ((), (), s32[]{:S(2)}) async-start(), calls=%async_computation.2 | async-start | bytes 3031040 | tf_op jit(solution)/shard_map/psum | solution.py:46
  24.6 3.1 %collective-permute-start = (f32[32,1]{1,0:T(8,128)S(1)}, f32[32,1]{1,0:T(8,128)S(1)}, u32[]{:S(2)}, u32[]{:S(2)}) collective-permute-start(f32[32,1]{1,0:T(8,128)S(1)} %bitcast.7), channel_id=1, source_target_pairs={{1,0},{3,2},{5,4},{7,6},{9,8},{11,10},{13,12},{15,14},{17,16},{19,... | collective-permute-start | bytes 392 | tf_op jit(solution)/shard_map/ppermute | solution.py:11
  111.7 140.7 %all-reduce.6.cloned.1.call-start = ((), (), s32[]{:S(2)}) async-start(), calls=%async_computation.1 | async-start | bytes 3031040 | tf_op jit(solution)/shard_map/psum | solution.py:46
  252.4 2.6 copy-start
Sparse Core Ops, SparseCore 0:
  9.5 11.7 all-gather.1
  111.8 16.2 all-reduce.7
  133.7 118.6 all-reduce.5
